TPU v7x, 32 devices: a whole 2x2x4 slice. The times are simulated.
32 devices in a mesh: roll: 4 (over x, core), tp: 8 (over z, y).
Axes of the slice: x: 2, y: 2, z: 4, core: 2. Of those that a mesh axis runs over, the one named last changes fastest.
Arguments:
- tokens: bfloat16 [128, 8, 2048], P(('roll', 'tp')), may hold values from -6 to 6
- lengths: int32 [128], P(('roll', 'tp')), may hold values from 1 to 8
- plan: int32 [2, 128, 1], P(None, ('roll', 'tp')), may hold values from 0 to 3, as said below
- owners: int32 [4], replicated, may hold values from 0 to 3, each once
- gate_up: float32 [4, 8, 2048, 768], P('roll', 'tp'), may hold values from -0.125 to 0.125
- down: float32 [4, 8, 384, 2048], P('roll', 'tp'), may hold values from -0.3125 to 0.3125
- norm_gain: float32 [2, 2048], replicated, may hold values from 0.5 to 1.5
- routing: int32 [2, 2048, 1], P(None, ('roll', 'tp')), may hold values from 0 to 7; in each aligned block of 64 rows (0 to 63, 64 to 127, ..., all dimensions but the last counted through in order) at most 10 rows name the same one
- route_weight: float32 [2, 2048], P(None, ('roll', 'tp')), may hold values from 0.1 to 1
Outputs:
- result: bfloat16 [128, 8, 2048], P(('roll', 'tp'))
Inputs may be any that keep to these rules, and one draw needn't show every extreme that they name: In layer 0 at most 2 rows of one device name the same owner, and every device's rows reach 2. For l >= 1, plan[l, i, 0] = (r + s_l[plan[l - 1, i, 0]]) mod 4, with r the roll index of row i's device and s_l a permutation of the owners drawn for layer l. owners is a permutation; layer l's master lies in the slot of roll index owners[l]. `routing`: every received token slot, empty ones included, names one window expert; of the 64 slots of one device at most 10 name the same expert, and in every draw some device reaches 10.
All inputs are finite; a program needn't handle non-finite values.
Results may differ from a plain program's by a relative error of at most 0.0048.
Values may be sent and summed in bfloat16 or wider, within the bound.
A program may use at most 128 MiB of HBM per device.

v0:
```python
import jax
import jax.numpy as jnp
from jax import lax
from jax.sharding import PartitionSpec as P

CAP = 2
epsilon = 1e-06


def spread(block, axis, owner):
    block = jnp.where(lax.axis_index(axis) == owner, block, jnp.zeros_like(block))
    return lax.psum(block, axis)


def slot_plan(target, groups, capacity):
    count = target.shape[0]
    earlier = jnp.arange(count)[None, :] < jnp.arange(count)[:, None]
    same = target[:, None] == target[None, :]
    within = jnp.sum(jnp.logical_and(same, earlier).astype(jnp.int32), axis=1)
    slot = target * capacity + within
    return (jnp.arange(groups * capacity)[:, None] == slot[None, :]).astype(jnp.bfloat16)


def into_slots(taken, items):
    flat = items.reshape(items.shape[0], -1)
    placed = jnp.dot(taken, flat, preferred_element_type=jnp.float32).astype(items.dtype)
    return placed.reshape((-1,) + items.shape[1:])


def from_slots(taken, slots):
    return into_slots(taken.T, slots)


def swap(value, distance):
    size = lax.axis_size("roll")
    return lax.ppermute(value, "roll", [(place, place ^ distance) for place in range(size)])


def share_halves(gate_up, down):
    upper = lax.rem(lax.axis_index("roll"), 2) == 1
    kept, given = ([], [])
    for master in (gate_up[0, 0], down[0, 0]):
        middle = master.shape[0] // 2
        low, high = (master[:middle].astype(jnp.bfloat16), master[middle:].astype(jnp.bfloat16))
        kept.append(jnp.where(upper, high, low))
        given.append(jnp.where(upper, low, high))
    return (kept, [swap(half, 1) for half in given])


def cross(kept, got, owner, before):
    me = lax.axis_index("roll")
    halves = [
        jnp.where(owner == me, mine, jnp.where(owner == me ^ 1, theirs, jnp.zeros_like(mine)))
        for mine, theirs in zip(kept, got)
    ]
    halves, _ = lax.optimization_barrier((halves, before))
    others = [jnp.zeros_like(half) for half in halves]
    distance = 2
    while distance < lax.axis_size("roll"):
        halves = [half + other for half, other in zip(halves, others)] if distance > 2 else halves
        others = [swap(half, distance) for half in halves]
        distance *= 2
    return (halves, others)


def complete(halves, others):
    upper = lax.rem(lax.axis_index("roll"), 2) == 1
    weights = []
    for half, other in zip(halves, others):
        half = half + other
        other = swap(half, 1)
        weights.append(
            jnp.concatenate([jnp.where(upper, other, half), jnp.where(upper, half, other)], axis=0)
        )
    return weights


def share_plan(plan, lengths, roll_size):
    layer_count, rows_dev = (plan.shape[0], plan.shape[1])
    packed = jnp.concatenate([plan[:, :, 0].reshape(-1), lengths])
    sent = jnp.broadcast_to(packed[None, :], (roll_size, packed.shape[0]))
    got = lax.all_to_all(sent, "roll", split_axis=0, concat_axis=0, tiled=True)
    return (got[:, :-rows_dev].reshape(roll_size, layer_count, rows_dev), got[:, -rows_dev:])


def held_lengths(owner, row_lengths):
    me, count = (lax.axis_index("roll"), owner.shape[1])
    earlier = jnp.arange(count)[None, :] < jnp.arange(count)[:, None]
    same = owner[:, :, None] == owner[:, None, :]
    within = jnp.sum(jnp.logical_and(same, earlier[None]).astype(jnp.int32), axis=2)
    here = jnp.logical_and(
        (owner == me)[:, None, :], within[:, None, :] == jnp.arange(CAP)[None, :, None]
    )
    return jnp.sum(jnp.where(here, row_lengths[:, None, :], 0), axis=2).reshape(-1)


def forward_plan(previous, owner, roll_size):
    me = lax.axis_index("roll")
    homes = jnp.arange(roll_size)
    turned = lax.rem(owner - homes[:, None] + roll_size, roll_size)
    turn = jnp.max(
        jnp.where(previous[:, :, None] == homes[None, None, :], turned[:, :, None], -1), axis=(0, 1)
    )
    mine = jnp.max(jnp.where(homes == me, turn, -1))
    to_send = jnp.logical_and(
        mine >= 0, homes[:, None] == lax.rem(homes[None, :] + mine, roll_size)
    )
    to_keep = jnp.logical_and(
        turn[None, :] >= 0, lax.rem(homes[:, None] + turn[None, :], roll_size) == me
    )
    return (to_send.astype(jnp.bfloat16), to_keep.astype(jnp.bfloat16))


def forward_rows(combined, moves, roll_size):
    chunks = into_slots(moves[0], combined.reshape((roll_size, CAP) + combined.shape[1:]))
    came = lax.all_to_all(chunks, "roll", split_axis=0, concat_axis=0, tiled=True)
    return into_slots(moves[1], came).reshape(combined.shape)


def send_home(combined, taken):
    home_rows = lax.all_to_all(combined, "roll", split_axis=0, concat_axis=0, tiled=True)
    return from_slots(taken, home_rows)


def process_rows(held, slot_lengths, crossing, first, layer_gain, route_column, weight_column):
    tp_size = lax.axis_size("tp")
    row_tokens = held.shape[1]
    model_width = held.shape[2]
    received = held.reshape(-1, model_width)
    token_count = received.shape[0]
    present = (jnp.arange(row_tokens)[None, :] < slot_lengths[:, None]).reshape(-1)
    widened = received.astype(jnp.float32)
    normed = (
        widened
        * lax.rsqrt(jnp.mean(widened * widened, axis=1, keepdims=True) + epsilon)
        * layer_gain[None, :]
    ).astype(jnp.bfloat16)
    expert_slots = 5 * token_count // (4 * tp_size)
    taken = slot_plan(route_column, tp_size, expert_slots)
    send_tokens = into_slots(taken, normed).reshape(tp_size, expert_slots, model_width)
    arrived = lax.all_to_all(send_tokens, "tp", split_axis=0, concat_axis=0, tiled=True)
    halves, others = crossing
    if first:
        others, arrived = lax.optimization_barrier((others, arrived))
    gate_up_w, down_w = complete(halves, others)
    hidden_width = down_w.shape[0]
    flattened = arrived.reshape(-1, model_width)
    projected = jnp.dot(flattened, gate_up_w, preferred_element_type=jnp.float32)
    hidden = (jax.nn.silu(projected[:, :hidden_width]) * projected[:, hidden_width:]).astype(
        jnp.bfloat16
    )
    produced = jnp.dot(hidden, down_w, preferred_element_type=jnp.float32).astype(jnp.bfloat16)
    returned = lax.all_to_all(
        produced.reshape(arrived.shape), "tp", split_axis=0, concat_axis=0, tiled=True
    )
    answer = from_slots(taken, returned.reshape(-1, model_width))
    combined = (
        widened
        + (present.astype(jnp.float32) * weight_column)[:, None] * answer.astype(jnp.float32)
    ).astype(jnp.bfloat16)
    return combined.reshape(held.shape)


def per_device(tokens, lengths, plan, owners, gate_up, down, norm_gain, routing, route_weight):
    layer_count = plan.shape[0]
    roll_size = lax.axis_size("roll")
    kept, got = share_halves(gate_up, down)
    home = slot_plan(plan[layer_count - 1, :, 0], roll_size, CAP)
    owner, row_lengths = share_plan(plan, lengths, roll_size)
    first_rows = into_slots(slot_plan(plan[0, :, 0], roll_size, CAP), tokens)
    held = lax.all_to_all(first_rows, "roll", split_axis=0, concat_axis=0, tiled=True)
    crossings, before = ([], (owner, row_lengths, held))
    for layer_index in range(layer_count):
        crossings.append(cross(kept, got, owners[layer_index], before))
        before = crossings[-1][1]
    for layer_index in range(layer_count):
        if layer_index > 0:
            moves = forward_plan(owner[:, layer_index - 1], owner[:, layer_index], roll_size)
            held = forward_rows(held, moves, roll_size)
        held = process_rows(
            held,
            held_lengths(owner[:, layer_index], row_lengths),
            crossings[layer_index],
            layer_index == 0,
            norm_gain[layer_index],
            routing[layer_index, :, 0],
            route_weight[layer_index],
        )
    current = send_home(held, home)
    return current


def solution(mesh):
    in_specs = (
        P(("roll", "tp"), None, None),
        P(("roll", "tp")),
        P(None, ("roll", "tp"), None),
        P(),
        P("roll", "tp", None, None),
        P("roll", "tp", None, None),
        P(),
        P(None, ("roll", "tp"), None),
        P(None, ("roll", "tp")),
    )
    out_specs = P(("roll", "tp"), None, None)
    return jax.shard_map(
        per_device, mesh=mesh, in_specs=in_specs, out_specs=out_specs, check_vma=False
    )
```

profile of v0, /device:TPU:0, one launch (start us, length us, event | category | flops | bytes accessed | tf_op | source)
XLA Modules:
  0.0 201.8 jit_solution(14525525016751189502)
XLA Ops:
  0.0 0.5 broadcast.191
  0.5 1.3 reduce.4
  1.9 0.7 pad_add_fusion
  2.7 0.6 broadcast_in_dim.29
  3.2 4.2 %all-to-all-start = ((s32[4,1,12]{2,1,0:T(1,128)}), s32[4,1,12]{2,1,0:T(1,128)S(1)}, u32[]{:S(2)}, u32[]{:S(2)}) async-start(s32[4,1,12]{2,1,0:T(1,128)} %broadcast_in_dim.29), calls=%async_computation | async-start | bytes 4096 | tf_op jit(solution)/shard_map/all_to_all | solution.py:82
  7.5 2.3 %convert.11 = bf16[1,1,384,2048]{3,2,1,0:T(8,128)(2,1)S(1)} convert(f32[1,1,384,2048]{3,2,1,0:T(8,128)} %param.14) | non-fusion elementwise | flops 786432 | bytes 4718592 | tf_op jit(solution)/shard_map/convert.3
  9.7 1.0 select_bitcast_fusion.1
  10.7 0.4 copy-done
  11.2 0.5 collective-permute-start.1
  11.7 0.4 copy-done.1
  12.0 0.3 convert.10
  12.4 1.3 select_bitcast_fusion
  13.7 0.5 collective-permute-start
  14.4 0.6 fusion.75
  18.3 0.9 copy.15
  19.2 3.4 %all-to-all-start.1 = ((bf16[8,8,2048]{2,1,0:T(8,128)(2,1)}), bf16[8,8,2048]{2,1,0:T(8,128)(2,1)S(1)}, u32[]{:S(2)}, u32[]{:S(2)}) async-start(bf16[8,8,2048]{2,1,0:T(8,128)(2,1)} %copy.15), calls=%async_computation.1 | async-start | bytes 524288 | tf_op jit(solution)/shard_map/all_to_all | solution.py:171
  22.7 2.9 %bitcast_select_fusion.2 = (bf16[192,2048]{1,0:T(8,128)(2,1)}, bf16[192,2048]{1,0:T(8,128)(2,1)}) fusion(bf16[192,2048]{1,0:T(8,128)(2,1)} %collective-permute-done.1, pred[]{:T(512)S(6)} %eq.277, pred[]{:T(512)S(6)} %eq.276, bf16[1,1,384,2048]{3,2,1,0:T(8,128)(2,1)} %copy-done, pred[]{:T(512)S(6)} %eq.261, pred[]{:T(512)S(6)} %eq.262, pred[]{:T(512)S(6)} %eq.260), kind=kLoop, calls=%fused_computation.42 | loop fusion | flops 1966080 | bytes 3932165 | tf_op jit(solution)/shard_map/jit(_where)/select_n | solution.py:53
  25.7 3.3 %bitcast_select_fusion = (bf16[1024,768]{1,0:T(8,128)(2,1)}, bf16[1024,768]{1,0:T(8,128)(2,1)}) fusion(bf16[1024,768]{1,0:T(8,128)(2,1)} %collective-permute-done, pred[]{:T(512)S(6)} %eq.277, pred[]{:T(512)S(6)} %eq.276, bf16[1,1,2048,768]{3,2,1,0:T(8,128)(2,1)S(1)} %convert.10, pred[]{:T(512)S(6)} %eq.261, pred[]{:T(512)S(6)} %eq.262, pred[]{:T(512)S(6)} %eq.260), kind=kLoop, calls=%fused_computation.34 | loop fusion | flops 3932160 | bytes 7864325 | tf_op jit(solution)/shard_map/jit(_where)/select_n | solution.py:53
  29.0 2.0 collective-permute-start.2
  31.4 0.3 convolution_convert_fusion.7
  31.8 0.9 reshape.238
  32.7 6.3 %all-to-all-start.2 = ((bf16[8,10,2048]{2,1,0:T(8,128)(2,1)}), bf16[8,10,2048]{2,1,0:T(8,128)(2,1)S(1)}, u32[]{:S(2)}, u32[]{:S(2)}) async-start(bf16[8,10,2048]{2,1,0:T(8,128)(2,1)} %reshape.238), calls=%async_computation.2 | async-start | bytes 1048576 | tf_op jit(solution)/shard_map/all_to_all | solution.py:141
  38.9 14.5 %all-to-all-done.2 = bf16[8,10,2048]{2,1,0:T(8,128)(2,1)S(1)} async-done(((bf16[8,10,2048]{2,1,0:T(8,128)(2,1)}), bf16[8,10,2048]{2,1,0:T(8,128)(2,1)S(1)}, u32[]{:S(2)}, u32[]{:S(2)}) %all-to-all-start.2) | async-done | bytes 327712 | tf_op jit(solution)/shard_map/all_to_all | solution.py:141
  53.5 29.4 %collective-permute-done.3 = bf16[192,2048]{1,0:T(8,128)(2,1)S(1)} collective-permute-done((bf16[192,2048]{1,0:T(8,128)(2,1)}, bf16[192,2048]{1,0:T(8,128)(2,1)S(1)}, u32[]{:S(2)}, u32[]{:S(2)}) %collective-permute-start.3) | collective-permute-done | bytes 786464 | tf_op jit(solution)/shard_map/ppermute | solution.py:36
  82.8 0.9 copy-done.6
  83.8 1.9 add.108
  85.8 1.2 add.110
  86.9 0.5 collective-permute-start.5
  87.4 0.3 select_reduce_fusion
  88.2 1.9 reshape.239
  90.0 1.7 collective-permute-start.6
  91.7 1.5 broadcast_select_fusion.8
  93.2 1.7 broadcast_select_fusion.3
  94.9 0.6 fusion.1
  95.5 0.4 convolution_convert_fusion.6
  96.0 0.9 reshape.240
  96.9 6.3 %all-to-all-start.3 = ((bf16[8,10,2048]{2,1,0:T(8,128)(2,1)}), bf16[8,10,2048]{2,1,0:T(8,128)(2,1)}, u32[]{:S(2)}, u32[]{:S(2)}) async-start(bf16[8,10,2048]{2,1,0:T(8,128)(2,1)} %reshape.240), calls=%async_computation.3 | async-start | bytes 1048576 | tf_op jit(solution)/shard_map/all_to_all | solution.py:153
  103.1 0.6 fusion.63
  104.9 0.6 collective-permute-start.8
  105.5 0.7 compare_select_fusion
  106.1 21.3 %collective-permute-done.6 = bf16[1024,768]{1,0:T(8,128)(2,1)} collective-permute-done((bf16[1024,768]{1,0:T(8,128)(2,1)S(1)}, bf16[1024,768]{1,0:T(8,128)(2,1)}, u32[]{:S(2)}, u32[]{:S(2)}) %collective-permute-start.6) | collective-permute-done | bytes 1572896 | tf_op jit(solution)/shard_map/ppermute | solution.py:36
  127.4 1.8 add.114
  129.3 1.2 reshape.241
  130.5 0.3 fusion.16
  130.9 0.3 convolution_convert_fusion.1
  131.2 0.8 copy.32
  132.1 3.4 %all-to-all-start.4 = ((bf16[4,2,8,2048]{3,2,1,0:T(8,128)(2,1)}), bf16[4,2,8,2048]{3,2,1,0:T(8,128)(2,1)S(1)}, u32[]{:S(2)}, u32[]{:S(2)}) async-start(bf16[4,2,8,2048]{3,2,1,0:T(8,128)(2,1)} %bitcast.78), calls=%async_computation.4 | async-start | bytes 524288 | tf_op jit(solution)/shard_map/all_to_all | solution.py:116
  135.5 8.8 %collective-permute-done.8 = bf16[192,2048]{1,0:T(8,128)(2,1)} collective-permute-done((bf16[192,2048]{1,0:T(8,128)(2,1)}, bf16[192,2048]{1,0:T(8,128)(2,1)}, u32[]{:S(2)}, u32[]{:S(2)}) %collective-permute-start.8) | collective-permute-done | bytes 786464 | tf_op jit(solution)/shard_map/ppermute | solution.py:36
  144.3 1.6 add.116
  146.2 0.3 fusion
  146.5 0.4 reshape.252
  147.1 0.3 convolution_convert_fusion.5
  147.4 0.9 reshape.244
  148.3 6.3 %all-to-all-start.5 = ((bf16[8,10,2048]{2,1,0:T(8,128)(2,1)}), bf16[8,10,2048]{2,1,0:T(8,128)(2,1)S(1)}, u32[]{:S(2)}, u32[]{:S(2)}) async-start(bf16[8,10,2048]{2,1,0:T(8,128)(2,1)} %reshape.244), calls=%async_computation.5 | async-start | bytes 1048576 | tf_op jit(solution)/shard_map/all_to_all | solution.py:141
  154.6 2.4 %broadcast_select_fusion.6 = (bf16[192,2048]{1,0:T(8,128)(2,1)}, bf16[192,2048]{1,0:T(8,128)(2,1)}) fusion(bf16[192,2048]{1,0:T(8,128)(2,1)} %collective-permute-done.9, bf16[192,2048]{1,0:T(8,128)(2,1)S(1)} %add.116, pred[]{:T(512)S(6)} %eq.261), kind=kLoop, calls=%fused_computation.46 | loop fusion | flops 786432 | bytes 3145729 | tf_op jit(solution)/shard_map/jit(_where)/select_n | solution.py:73
  157.0 12.7 %all-to-all-done.5 = bf16[8,10,2048]{2,1,0:T(8,128)(2,1)S(1)} async-done(((bf16[8,10,2048]{2,1,0:T(8,128)(2,1)}), bf16[8,10,2048]{2,1,0:T(8,128)(2,1)S(1)}, u32[]{:S(2)}, u32[]{:S(2)}) %all-to-all-start.5) | async-done | bytes 327712 | tf_op jit(solution)/shard_map/all_to_all | solution.py:141
  169.8 1.6 broadcast_select_fusion.1
  171.4 0.6 fusion.5
  172.1 0.5 copy-done.8
  172.8 0.4 convolution_convert_fusion.4
  173.4 18.1 %all_to_all.44 = bf16[8,10,2048]{2,1,0:T(8,128)(2,1)S(1)} all-to-all(bf16[8,10,2048]{2,1,0:T(8,128)(2,1)S(1)} %reshape.246), channel_id=1, replica_groups=mesh['roll'=4,'tp'=8] {'tp'}, dimensions={0} | all-to-all | bytes 655360 | tf_op jit(solution)/shard_map/all_to_all | solution.py:153
  191.6 0.3 fusion.17
  191.9 8.8 %all_to_all.45 = bf16[8,8,2048]{2,1,0:T(8,128)(2,1)S(1)} all-to-all(bf16[8,8,2048]{2,1,0:T(8,128)(2,1)S(1)} %fusion.17), channel_id=1, replica_groups=mesh['roll'=4,'tp'=8] {'roll'}, dimensions={0} | all-to-all | bytes 524288 | tf_op jit(solution)/shard_map/all_to_all | solution.py:121
  201.1 0.7 copy.33
  (87 shorter events, 4.2 us)
Async XLA Ops:
  3.2 15.9 %all-to-all-start = ((s32[4,1,12]{2,1,0:T(1,128)}), s32[4,1,12]{2,1,0:T(1,128)S(1)}, u32[]{:S(2)}, u32[]{:S(2)}) async-start(s32[4,1,12]{2,1,0:T(1,128)} %broadcast_in_dim.29), calls=%async_computation | async-start | bytes 4096 | tf_op jit(solution)/shard_map/all_to_all | solution.py:82
  7.5 4.6 %copy-start.1 = (f32[1,1,2048,768]{3,2,1,0:T(8,128)S(1)}, f32[1,1,2048,768]{3,2,1,0:T(8,128)}, u32[]{:S(2)}) copy-start(f32[1,1,2048,768]{3,2,1,0:T(8,128)} %param.13) | copy-start | bytes 18874372
  9.7 1.4 copy-start
  11.2 11.6 %collective-permute-start.1 = (bf16[192,2048]{1,0:T(8,128)(2,1)}, bf16[192,2048]{1,0:T(8,128)(2,1)}, u32[]{:S(2)}, u32[]{:S(2)}) collective-permute-start(bf16[192,2048]{1,0:T(8,128)(2,1)} %select_bitcast_fusion.1), channel_id=1, source_target_pairs={{0,8},{8,0},{16,24},{24,16},{1,9},{9,1},{17,25},{25,17},{2,10},{10... | collective-permute-start | bytes 2359304 | tf_op jit(solution)/shard_map/ppermute | solution.py:36
  12.3 1.9 copy-start.14
  12.4 2.1 %copy-start.15 = (s32[4]{0:T(128)S(1)}, s32[4]{0:T(128)}, u32[]{:S(2)}) copy-start(s32[4]{0:T(128)} %param.12) | copy-start | bytes 52
  12.4 5.3 %copy-start.11 = (bf16[4,8,2048]{2,1,0:T(8,128)(2,1)S(1)}, bf16[4,8,2048]{2,1,0:T(8,128)(2,1)}, u32[]{:S(2)}) copy-start(bf16[4,8,2048]{2,1,0:T(8,128)(2,1)} %param.9) | copy-start | bytes 393220
  12.4 5.4 %copy-start.13 = (s32[2,4,1]{1,2,0:T(1,128)S(1)}, s32[2,4,1]{1,2,0:T(1,128)}, u32[]{:S(2)}) copy-start(s32[2,4,1]{1,2,0:T(1,128)} %param.11) | copy-start | bytes 100
  13.7 11.9 %collective-permute-start = (bf16[1024,768]{1,0:T(8,128)(2,1)}, bf16[1024,768]{1,0:T(8,128)(2,1)}, u32[]{:S(2)}, u32[]{:S(2)}) collective-permute-start(bf16[1024,768]{1,0:T(8,128)(2,1)} %select_bitcast_fusion), channel_id=1, source_target_pairs={{0,8},{8,0},{16,24},{24,16},{1,9},{9,1},{17,25},{25,17},{2,10},{10... | collective-permute-start | bytes 4718600 | tf_op jit(solution)/shard_map/ppermute | solution.py:36
  19.2 9.9 %all-to-all-start.1 = ((bf16[8,8,2048]{2,1,0:T(8,128)(2,1)}), bf16[8,8,2048]{2,1,0:T(8,128)(2,1)S(1)}, u32[]{:S(2)}, u32[]{:S(2)}) async-start(bf16[8,8,2048]{2,1,0:T(8,128)(2,1)} %copy.15), calls=%async_computation.1 | async-start | bytes 524288 | tf_op jit(solution)/shard_map/all_to_all | solution.py:171
  25.7 5.3 %copy-start.12 = (f32[2,2048]{1,0:T(2,128)S(1)}, f32[2,2048]{1,0:T(2,128)}, u32[]{:S(2)}) copy-start(f32[2,2048]{1,0:T(2,128)} %param.15) | copy-start | bytes 49156
  29.0 54.8 %copy-start.3 = (bf16[1024,768]{1,0:T(8,128)(2,1)S(1)}, bf16[1024,768]{1,0:T(8,128)(2,1)}, u32[]{:S(2)}) copy-start(bf16[1024,768]{1,0:T(8,128)(2,1)} %get-tuple-element.12) | copy-start | bytes 4718596
  29.0 54.8 %collective-permute-start.2 = (bf16[1024,768]{1,0:T(8,128)(2,1)}, bf16[1024,768]{1,0:T(8,128)(2,1)}, u32[]{:S(2)}, u32[]{:S(2)}) collective-permute-start(bf16[1024,768]{1,0:T(8,128)(2,1)} %get-tuple-element.12), channel_id=1, source_target_pairs={{0,16},{8,24},{16,0},{24,8},{1,17},{9,25},{17,1},{25,9},{2,18},{10... | collective-permute-start | bytes 4718600 | tf_op jit(solution)/shard_map/ppermute | solution.py:36
  31.4 51.5 %collective-permute-start.3 = (bf16[192,2048]{1,0:T(8,128)(2,1)}, bf16[192,2048]{1,0:T(8,128)(2,1)S(1)}, u32[]{:S(2)}, u32[]{:S(2)}) collective-permute-start(bf16[192,2048]{1,0:T(8,128)(2,1)} %get-tuple-element.13), channel_id=1, source_target_pairs={{0,16},{8,24},{16,0},{24,8},{1,17},{9,25},{17,1},{25,9},{2,18},{10... | collective-permute-start | bytes 2359304 | tf_op jit(solution)/shard_map/ppermute | solution.py:36
  32.7 20.8 %all-to-all-start.2 = ((bf16[8,10,2048]{2,1,0:T(8,128)(2,1)}), bf16[8,10,2048]{2,1,0:T(8,128)(2,1)S(1)}, u32[]{:S(2)}, u32[]{:S(2)}) async-start(bf16[8,10,2048]{2,1,0:T(8,128)(2,1)} %reshape.238), calls=%async_computation.2 | async-start | bytes 1048576 | tf_op jit(solution)/shard_map/all_to_all | solution.py:141
  53.5 29.4 %copy-start.5 = (bf16[8,10,2048]{2,1,0:T(8,128)(2,1)}, bf16[8,10,2048]{2,1,0:T(8,128)(2,1)S(1)}, u32[]{:S(2)}) copy-start(bf16[8,10,2048]{2,1,0:T(8,128)(2,1)S(1)} %all-to-all-done.2) | copy-start | bytes 983044
  53.5 32.2 %copy-start.4 = (bf16[192,2048]{1,0:T(8,128)(2,1)S(1)}, bf16[192,2048]{1,0:T(8,128)(2,1)}, u32[]{:S(2)}) copy-start(bf16[192,2048]{1,0:T(8,128)(2,1)} %get-tuple-element.13) | copy-start | bytes 2359300
  82.8 0.9 copy-start.6
  83.8 2.0 copy-start.7
  85.6 7.6 %collective-permute-start.4 = (bf16[1024,768]{1,0:T(8,128)(2,1)S(1)}, bf16[1024,768]{1,0:T(8,128)(2,1)}, u32[]{:S(2)}, u32[]{:S(2)}) collective-permute-start(bf16[1024,768]{1,0:T(8,128)(2,1)S(1)} %add.108), channel_id=1, source_target_pairs={{0,8},{8,0},{16,24},{24,16},{1,9},{9,1},{17,25},{25,17},{2,10},{10... | collective-permute-start | bytes 4718600 | tf_op jit(solution)/shard_map/ppermute | solution.py:36
  85.8 4.3 %copy-start.2 = (bf16[1024,768]{1,0:T(8,128)(2,1)S(1)}, bf16[1024,768]{1,0:T(8,128)(2,1)}, u32[]{:S(2)}) copy-start(bf16[1024,768]{1,0:T(8,128)(2,1)} %get-tuple-element.17) | copy-start | bytes 4718596
  86.9 4.8 %collective-permute-start.5 = (bf16[192,2048]{1,0:T(8,128)(2,1)}, bf16[192,2048]{1,0:T(8,128)(2,1)}, u32[]{:S(2)}, u32[]{:S(2)}) collective-permute-start(bf16[192,2048]{1,0:T(8,128)(2,1)} %add.110), channel_id=1, source_target_pairs={{0,8},{8,0},{16,24},{24,16},{1,9},{9,1},{17,25},{25,17},{2,10},{10... | collective-permute-start | bytes 2359304 | tf_op jit(solution)/shard_map/ppermute | solution.py:36
  90.0 37.4 %collective-permute-start.6 = (bf16[1024,768]{1,0:T(8,128)(2,1)S(1)}, bf16[1024,768]{1,0:T(8,128)(2,1)}, u32[]{:S(2)}, u32[]{:S(2)}) collective-permute-start(bf16[1024,768]{1,0:T(8,128)(2,1)S(1)} %copy-done.2), channel_id=1, source_target_pairs={{0,16},{8,24},{16,0},{24,8},{1,17},{9,25},{17,1},{25,9},{2,18},{10... | collective-permute-start | bytes 4718600 | tf_op jit(solution)/shard_map/ppermute | solution.py:36
  93.2 1.7 copy-start.10
  96.0 8.9 %copy-start.16 = (f32[2,64]{1,0:T(2,128)S(1)}, f32[2,64]{1,0:T(2,128)}, u32[]{:S(2)}) copy-start(f32[2,64]{1,0:T(2,128)} %param.17) | copy-start | bytes 1540
  96.9 32.4 %all-to-all-start.3 = ((bf16[8,10,2048]{2,1,0:T(8,128)(2,1)}), bf16[8,10,2048]{2,1,0:T(8,128)(2,1)}, u32[]{:S(2)}, u32[]{:S(2)}) async-start(bf16[8,10,2048]{2,1,0:T(8,128)(2,1)} %reshape.240), calls=%async_computation.3 | async-start | bytes 1048576 | tf_op jit(solution)/shard_map/all_to_all | solution.py:153
  104.9 39.4 %collective-permute-start.8 = (bf16[192,2048]{1,0:T(8,128)(2,1)}, bf16[192,2048]{1,0:T(8,128)(2,1)}, u32[]{:S(2)}, u32[]{:S(2)}) collective-permute-start(bf16[192,2048]{1,0:T(8,128)(2,1)} %get-tuple-element.18), channel_id=1, source_target_pairs={{0,16},{8,24},{16,0},{24,8},{1,17},{9,25},{17,1},{25,9},{2,18},{10... | collective-permute-start | bytes 2359304 | tf_op jit(solution)/shard_map/ppermute | solution.py:36
  129.2 40.6 %collective-permute-start.7 = (bf16[1024,768]{1,0:T(8,128)(2,1)S(1)}, bf16[1024,768]{1,0:T(8,128)(2,1)}, u32[]{:S(2)}, u32[]{:S(2)}) collective-permute-start(bf16[1024,768]{1,0:T(8,128)(2,1)S(1)} %add.114), channel_id=1, source_target_pairs={{0,8},{8,0},{16,24},{24,16},{1,9},{9,1},{17,25},{25,17},{2,10},{10... | collective-permute-start | bytes 4718600 | tf_op jit(solution)/shard_map/ppermute | solution.py:36
  132.1 14.0 %all-to-all-start.4 = ((bf16[4,2,8,2048]{3,2,1,0:T(8,128)(2,1)}), bf16[4,2,8,2048]{3,2,1,0:T(8,128)(2,1)S(1)}, u32[]{:S(2)}, u32[]{:S(2)}) async-start(bf16[4,2,8,2048]{3,2,1,0:T(8,128)(2,1)} %bitcast.78), calls=%async_computation.4 | async-start | bytes 524288 | tf_op jit(solution)/shard_map/all_to_all | solution.py:116
  145.9 8.7 %collective-permute-start.9 = (bf16[192,2048]{1,0:T(8,128)(2,1)S(1)}, bf16[192,2048]{1,0:T(8,128)(2,1)}, u32[]{:S(2)}, u32[]{:S(2)}) collective-permute-start(bf16[192,2048]{1,0:T(8,128)(2,1)S(1)} %add.116), channel_id=1, source_target_pairs={{0,8},{8,0},{16,24},{24,16},{1,9},{9,1},{17,25},{25,17},{2,10},{10... | collective-permute-start | bytes 2359304 | tf_op jit(solution)/shard_map/ppermute | solution.py:36
  148.3 21.4 %all-to-all-start.5 = ((bf16[8,10,2048]{2,1,0:T(8,128)(2,1)}), bf16[8,10,2048]{2,1,0:T(8,128)(2,1)S(1)}, u32[]{:S(2)}, u32[]{:S(2)}) async-start(bf16[8,10,2048]{2,1,0:T(8,128)(2,1)} %reshape.244), calls=%async_computation.5 | async-start | bytes 1048576 | tf_op jit(solution)/shard_map/all_to_all | solution.py:141
  171.4 1.1 copy-start.8
  171.4 1.4 copy-start.9
where the time goes:
time: 203 us; the launch traced here: 202 us
  waiting for transfers between devices  86.7 us (43%)
  starting transfers between devices  35.8 us (18%)
  other arithmetic  29.4 us (14%)
  blocking collectives  26.9 us (13%)
  local copies, waits for them, and re-layouts  14.8 us (7%)
  matrix products  4.39 us (2%)
  between operations  3.76 us (2%)
    ppermute x10, waiting for transfers between devices, swap(): lax.ppermute(value, 'roll', [(place, place ^ distance) for place in range...  59.4 us
    all_to_all x2, waiting for transfers between devices, process_rows(): lax.all_to_all(send_tokens, 'tp', split_axis=0, concat_axis=0, tiled=True)  27.2 us
    all_to_all x1, blocking collectives, process_rows(): lax.all_to_all(produced.reshape(arrived.shape), 'tp', split_axis=0, conca...  18.1 us
    all_to_all x2, starting transfers between devices, process_rows(): lax.all_to_all(send_tokens, 'tp', split_axis=0, concat_axis=0, tiled=True)  12.5 us
    all_to_all x1, blocking collectives, send_home(): lax.all_to_all(combined, 'roll', split_axis=0, concat_axis=0, tiled=True)  8.77 us
    select_n x4, other arithmetic, complete(): jnp.where(upper, other, half)  7.14 us
    add x4, other arithmetic, complete(): half = half + other  6.47 us
    select_n x2, other arithmetic, cross(): jnp.where(owner == me, mine, jnp.where(owner == me ^ 1, theirs, jnp.zeros...  6.27 us
  transfers between devices with their start and end apart: 16, of which 6 were waited for; matrix products, arithmetic and copies ran while one was open for 18% of the time, Pallas kernels for 0%

commit v1 on v0

--- a/solution.py
+++ b/solution.py
@@ -1,3 +1,4 @@
+import functools
 import jax
 import jax.numpy as jnp
 from jax import lax
@@ -5,6 +6,42 @@
 
 CAP = 2
 epsilon = 1e-06
+
+
+def object_divide(q_in, along_dim, body):
+    current_block = q_in.shape
+    b_now = q_in.reshape(
+        *current_block[:along_dim],
+        body,
+        current_block[along_dim] // body,
+        *current_block[along_dim + 1 :]
+    )
+    return jnp.moveaxis(b_now, along_dim, 0)
+
+
+def update_case_all(block_in, in_dim):
+    vec_out = list(block_in.shape[1:])
+    vec_out[in_dim] *= block_in.shape[0]
+    return jnp.moveaxis(block_in, 0, in_dim).reshape(vec_out)
+
+
+def balance_joints_up(local_values, named_axis, x_local, z):
+    long_array = lax.axis_size(named_axis)
+    piece_now = lax.axis_index(named_axis)
+    side_arr, extra = (long_array, piece_now)
+    out_arr = object_divide(local_values, x_local, side_arr)
+    so_far_all = [out_arr[extra]]
+    for c in range(1, side_arr):
+        view_out = out_arr[(extra + c) % side_arr]
+        state_now = lax.ppermute(
+            view_out, named_axis, [(j0, (j0 + c) % side_arr) for j0 in range(side_arr)]
+        )
+        so_far_all.append(state_now)
+    out_arr = jnp.stack(so_far_all)[(extra - jnp.arange(side_arr)) % side_arr]
+    return update_case_all(out_arr, z)
+
+
+lift_the_scenes = functools.partial(balance_joints_up, named_axis="tp", x_local=0, z=0)
 
 
 def spread(block, axis, owner):
@@ -150,9 +187,7 @@
         jnp.bfloat16
     )
     produced = jnp.dot(hidden, down_w, preferred_element_type=jnp.float32).astype(jnp.bfloat16)
-    returned = lax.all_to_all(
-        produced.reshape(arrived.shape), "tp", split_axis=0, concat_axis=0, tiled=True
-    )
+    returned = lift_the_scenes(produced.reshape(arrived.shape))
     answer = from_slots(taken, returned.reshape(-1, model_width))
     combined = (
         widened

time: 203 us -> 227 us (1.12)
  waiting for transfers between devices: 86.7 us -> 109 us
  blocking collectives: 26.9 us -> 8.42 us
  starting transfers between devices: 35.8 us -> 48.5 us
  local copies, waits for them, and re-layouts: 14.8 us -> 19.8 us
    ppermute x0 -> x14, waiting for transfers between devices: none -> 27.5 us  [balance_joints_up(): lax.ppermute(view_out, named_axis, [(j0, (j0 + c) % side_arr) for j0 in r...]
    ppermute x0 -> x14, starting transfers between devices: none -> 20.8 us  [balance_joints_up(): lax.ppermute(view_out, named_axis, [(j0, (j0 + c) % side_arr) for j0 in r...]
    all_to_all x1 -> x0, blocking collectives: 18.1 us -> none  [process_rows(): lax.all_to_all(produced.reshape(arrived.shape), 'tp', split_axis=0, conca...]
    ppermute x10, waiting for transfers between devices: 59.4 us -> 50.7 us  [swap(): lax.ppermute(value, 'roll', [(place, place ^ distance) for place in range...]
    all_to_all x1 -> x0, starting transfers between devices: 6.27 us -> none  [process_rows(): lax.all_to_all(produced.reshape(arrived.shape), 'tp', split_axis=0, conca...]
    all_to_all x1, waiting for transfers between devices: 0.06 us -> 3.77 us  [forward_rows(): lax.all_to_all(chunks, 'roll', split_axis=0, concat_axis=0, tiled=True)]
    reshape x4 -> x0, local copies, waits for them, and re-layouts: 2.28 us -> none  [the longest x2 1.28 us: process_rows(): answer = from_slots(taken, returned.reshape(-1, model_width))]
    unnamed x42 -> x78, local copies, waits for them, and re-layouts: 5.13 us -> 6.82 us
  transfers between devices with their start and end apart: 16 -> 29, of which waited for: 6 -> 10; matrix products, arithmetic and copies ran while one was open for 18% -> 19% of each run, Pallas kernels for 0% -> 0%
where the time goes in v1:
time: 227 us; the launch traced here: 226 us
  waiting for transfers between devices  109 us (48%)
  starting transfers between devices  48.5 us (21%)
  other arithmetic  31.3 us (14%)
  local copies, waits for them, and re-layouts  19.8 us (9%)
  blocking collectives  8.42 us (4%)
  matrix products  5.2 us (2%)
  between operations  3.81 us (2%)
    ppermute x10, waiting for transfers between devices, swap(): lax.ppermute(value, 'roll', [(place, place ^ distance) for place in range...  50.7 us
    ppermute x14, waiting for transfers between devices, balance_joints_up(): lax.ppermute(view_out, named_axis, [(j0, (j0 + c) % side_arr) for j0 in r...  27.5 us
    all_to_all x2, waiting for transfers between devices, process_rows(): lax.all_to_all(send_tokens, 'tp', split_axis=0, concat_axis=0, tiled=True)  26.8 us
    ppermute x14, starting transfers between devices, balance_joints_up(): lax.ppermute(view_out, named_axis, [(j0, (j0 + c) % side_arr) for j0 in r...  20.8 us
    all_to_all x2, starting transfers between devices, process_rows(): lax.all_to_all(send_tokens, 'tp', split_axis=0, concat_axis=0, tiled=True)  10.4 us
    all_to_all x1, blocking collectives, send_home(): lax.all_to_all(combined, 'roll', split_axis=0, concat_axis=0, tiled=True)  8.42 us
    select_n x4, other arithmetic, complete(): jnp.where(upper, other, half)  7.13 us
    unnamed x78, local copies, waits for them, and re-layouts  6.82 us
  transfers between devices with their start and end apart: 29, of which 10 were waited for; matrix products, arithmetic and copies ran while one was open for 19% of the time, Pallas kernels for 0%

profile of v1, /device:TPU:0, one launch (start us, length us, event | category | flops | bytes accessed | tf_op | source)
XLA Modules:
  0.0 225.7 jit_solution(16328000387018531007)
XLA Ops:
  0.5 1.3 reduce.4
  1.9 0.7 pad_add_fusion
  2.7 0.6 broadcast_in_dim.29
  3.2 4.2 %all-to-all-start = ((s32[4,1,12]{2,1,0:T(1,128)}), s32[4,1,12]{2,1,0:T(1,128)S(1)}, u32[]{:S(2)}, u32[]{:S(2)}) async-start(s32[4,1,12]{2,1,0:T(1,128)} %broadcast_in_dim.29), calls=%async_computation | async-start | bytes 4096 | tf_op jit(solution)/shard_map/all_to_all | solution.py:119
  7.5 2.3 convert.11
  9.7 1.0 select_bitcast_fusion.1
  12.4 1.3 select_bitcast_fusion
  14.5 0.6 fusion.76
  18.3 0.6 multiply_add_fusion.3
  19.0 0.9 copy.15
  19.9 3.4 %all-to-all-start.1 = ((bf16[8,8,2048]{2,1,0:T(8,128)(2,1)}), bf16[8,8,2048]{2,1,0:T(8,128)(2,1)S(1)}, u32[]{:S(2)}, u32[]{:S(2)}) async-start(bf16[8,8,2048]{2,1,0:T(8,128)(2,1)} %copy.15), calls=%async_computation.1 | async-start | bytes 524288 | tf_op jit(solution)/shard_map/all_to_all | solution.py:206
  23.3 2.9 %bitcast_select_fusion.2 = (bf16[192,2048]{1,0:T(8,128)(2,1)}, bf16[192,2048]{1,0:T(8,128)(2,1)}) fusion(bf16[192,2048]{1,0:T(8,128)(2,1)} %collective-permute-done.1, pred[]{:T(512)S(6)} %eq.295, pred[]{:T(512)S(6)} %eq.294, bf16[1,1,384,2048]{3,2,1,0:T(8,128)(2,1)} %copy-done, pred[]{:T(512)S(6)} %eq.279, pred[]{:T(512)S(6)} %eq.280, pred[]{:T(512)S(6)} %eq.278), kind=kLoop, calls=%fused_computation.44 | loop fusion | flops 1966080 | bytes 3932165 | tf_op jit(solution)/shard_map/jit(_where)/select_n | solution.py:90
  26.3 3.4 %bitcast_select_fusion = (bf16[1024,768]{1,0:T(8,128)(2,1)}, bf16[1024,768]{1,0:T(8,128)(2,1)}) fusion(bf16[1024,768]{1,0:T(8,128)(2,1)} %collective-permute-done, pred[]{:T(512)S(6)} %eq.295, pred[]{:T(512)S(6)} %eq.294, bf16[1,1,2048,768]{3,2,1,0:T(8,128)(2,1)S(1)} %convert.10, pred[]{:T(512)S(6)} %eq.279, pred[]{:T(512)S(6)} %eq.280, pred[]{:T(512)S(6)} %eq.278), kind=kLoop, calls=%fused_computation.36 | loop fusion | flops 3932160 | bytes 7864325 | tf_op jit(solution)/shard_map/jit(_where)/select_n | solution.py:90
  29.6 2.0 collective-permute-start.2
  32.4 0.9 reshape.275
  33.3 6.3 %all-to-all-start.2 = ((bf16[8,10,2048]{2,1,0:T(8,128)(2,1)}), bf16[8,10,2048]{2,1,0:T(8,128)(2,1)}, u32[]{:S(2)}, u32[]{:S(2)}) async-start(bf16[8,10,2048]{2,1,0:T(8,128)(2,1)} %reshape.275), calls=%async_computation.2 | async-start | bytes 1048576 | tf_op jit(solution)/shard_map/all_to_all | solution.py:178
  39.6 14.6 %all-to-all-done.2 = bf16[8,10,2048]{2,1,0:T(8,128)(2,1)} async-done(((bf16[8,10,2048]{2,1,0:T(8,128)(2,1)}), bf16[8,10,2048]{2,1,0:T(8,128)(2,1)}, u32[]{:S(2)}, u32[]{:S(2)}) %all-to-all-start.2) | async-done | bytes 327712 | tf_op jit(solution)/shard_map/all_to_all | solution.py:178
  54.2 29.2 %collective-permute-done.3 = bf16[192,2048]{1,0:T(8,128)(2,1)S(1)} collective-permute-done((bf16[192,2048]{1,0:T(8,128)(2,1)}, bf16[192,2048]{1,0:T(8,128)(2,1)S(1)}, u32[]{:S(2)}, u32[]{:S(2)}) %collective-permute-start.3) | collective-permute-done | bytes 786464 | tf_op jit(solution)/shard_map/ppermute | solution.py:73
  83.5 0.9 copy-done.5
  84.3 1.9 add.223
  86.7 1.2 add.225
  89.1 0.6 fusion.63
  89.8 0.6 bitcast_select_fusion.4
  90.3 1.9 reshape.276
  92.2 1.7 collective-permute-start.13
  93.9 1.5 broadcast_select_fusion.8
  95.4 1.7 broadcast_select_fusion.3
  97.1 0.6 fusion.1
  98.3 0.8 dynamic-slice_bitcast_fusion.7
  99.0 1.9 collective-permute-start.6
  101.0 1.1 compare_select_fusion.3
  103.1 3.0 %collective-permute-start.12 = (bf16[1,10,2048]{2,1,0:T(8,128)(2,1)S(1)}, bf16[1,10,2048]{2,1,0:T(8,128)(2,1)S(1)}, u32[]{:S(2)}, u32[]{:S(2)}) collective-permute-start(bf16[1,10,2048]{2,1,0:T(8,128)(2,1)S(1)} %get-tuple-element.44), channel_id=1, source_target_pairs={{0,7},{1,0},{2,1},{3,2},{4,3},{5,4},{6,5},{7,6},{8,15},{9,8},{10,9... | collective-permute-start | bytes 122888 | tf_op jit(solution)/shard_map/ppermute | solution.py:36
  106.2 2.0 collective-permute-start.11
  108.1 21.5 %collective-permute-done.13 = bf16[1024,768]{1,0:T(8,128)(2,1)} collective-permute-done((bf16[1024,768]{1,0:T(8,128)(2,1)S(1)}, bf16[1024,768]{1,0:T(8,128)(2,1)}, u32[]{:S(2)}, u32[]{:S(2)}) %collective-permute-start.13) | collective-permute-done | bytes 1572896 | tf_op jit(solution)/shard_map/ppermute | solution.py:73
  129.6 4.0 %collective-permute-start.10 = (bf16[1,10,2048]{2,1,0:T(8,128)(2,1)}, bf16[1,10,2048]{2,1,0:T(8,128)(2,1)S(1)}, u32[]{:S(2)}, u32[]{:S(2)}) collective-permute-start(bf16[1,10,2048]{2,1,0:T(8,128)(2,1)} %get-tuple-element.46), channel_id=1, source_target_pairs={{0,5},{1,6},{2,7},{3,0},{4,1},{5,2},{6,3},{7,4},{8,13},{9,14},{10,... | collective-permute-start | bytes 122888 | tf_op jit(solution)/shard_map/ppermute | solution.py:36
  133.6 1.8 add.253
  135.5 1.6 collective-permute-start.7
  137.1 0.8 bitcast_dynamic-update-slice_fusion.13
  138.0 3.6 %collective-permute-done.7 = bf16[1,10,2048]{2,1,0:T(8,128)(2,1)S(1)} collective-permute-done((bf16[1,10,2048]{2,1,0:T(8,128)(2,1)S(1)}, bf16[1,10,2048]{2,1,0:T(8,128)(2,1)S(1)}, u32[]{:S(2)}, u32[]{:S(2)}) %collective-permute-start.7) | collective-permute-done | bytes 40992 | tf_op jit(solution)/shard_map/ppermute | solution.py:36
  141.6 6.2 %collective-permute-done.8 = bf16[1,10,2048]{2,1,0:T(8,128)(2,1)S(1)} collective-permute-done((bf16[1,10,2048]{2,1,0:T(8,128)(2,1)S(1)}, bf16[1,10,2048]{2,1,0:T(8,128)(2,1)S(1)}, u32[]{:S(2)}, u32[]{:S(2)}) %collective-permute-start.8) | collective-permute-done | bytes 40992 | tf_op jit(solution)/shard_map/ppermute | solution.py:36
  147.8 5.2 %collective-permute-done.9 = bf16[1,10,2048]{2,1,0:T(8,128)(2,1)S(1)} collective-permute-done((bf16[1,10,2048]{2,1,0:T(8,128)(2,1)S(1)}, bf16[1,10,2048]{2,1,0:T(8,128)(2,1)S(1)}, u32[]{:S(2)}, u32[]{:S(2)}) %collective-permute-start.9) | collective-permute-done | bytes 40992 | tf_op jit(solution)/shard_map/ppermute | solution.py:36
  153.1 0.8 copy-done.10
  153.9 1.6 gather_fusion
  156.5 0.9 copy.32
  157.3 3.4 %all-to-all-start.3 = ((bf16[4,2,8,2048]{3,2,1,0:T(8,128)(2,1)}), bf16[4,2,8,2048]{3,2,1,0:T(8,128)(2,1)S(1)}, u32[]{:S(2)}, u32[]{:S(2)}) async-start(bf16[4,2,8,2048]{3,2,1,0:T(8,128)(2,1)} %bitcast.138), calls=%async_computation.3 | async-start | bytes 524288 | tf_op jit(solution)/shard_map/all_to_all | solution.py:153
  160.8 1.6 add.255
  163.0 3.8 %all-to-all-done.3 = bf16[4,2,8,2048]{3,2,1,0:T(8,128)(2,1)S(1)} async-done(((bf16[4,2,8,2048]{3,2,1,0:T(8,128)(2,1)}), bf16[4,2,8,2048]{3,2,1,0:T(8,128)(2,1)S(1)}, u32[]{:S(2)}, u32[]{:S(2)}) %all-to-all-start.3) | async-done | bytes 262176 | tf_op jit(solution)/shard_map/all_to_all | solution.py:153
  167.0 1.1 fusion
  168.0 1.4 reshape.285
  169.9 0.9 reshape.279
  170.9 4.1 %all-to-all-start.4 = ((bf16[8,10,2048]{2,1,0:T(8,128)(2,1)}), bf16[8,10,2048]{2,1,0:T(8,128)(2,1)}, u32[]{:S(2)}, u32[]{:S(2)}) async-start(bf16[8,10,2048]{2,1,0:T(8,128)(2,1)} %reshape.279), calls=%async_computation.4 | async-start | bytes 1048576 | tf_op jit(solution)/shard_map/all_to_all | solution.py:178
  175.0 2.4 %broadcast_select_fusion.6 = (bf16[192,2048]{1,0:T(8,128)(2,1)}, bf16[192,2048]{1,0:T(8,128)(2,1)}) fusion(bf16[192,2048]{1,0:T(8,128)(2,1)} %collective-permute-done.16, bf16[192,2048]{1,0:T(8,128)(2,1)S(1)} %add.255, pred[]{:T(512)S(6)} %eq.279), kind=kLoop, calls=%fused_computation.48 | loop fusion | flops 786432 | bytes 3145729 | tf_op jit(solution)/shard_map/jit(_where)/select_n | solution.py:110
  177.4 12.2 %all-to-all-done.4 = bf16[8,10,2048]{2,1,0:T(8,128)(2,1)} async-done(((bf16[8,10,2048]{2,1,0:T(8,128)(2,1)}), bf16[8,10,2048]{2,1,0:T(8,128)(2,1)}, u32[]{:S(2)}, u32[]{:S(2)}) %all-to-all-start.4) | async-done | bytes 327712 | tf_op jit(solution)/shard_map/all_to_all | solution.py:178
  189.6 1.2 reshape.280
  190.7 1.6 broadcast_select_fusion.1
  192.4 0.6 fusion.5
  194.4 1.5 collective-permute-start.17
  195.9 3.3 %collective-permute-start.23 = (bf16[1,10,2048]{2,1,0:T(8,128)(2,1)S(1)}, bf16[1,10,2048]{2,1,0:T(8,128)(2,1)S(1)}, u32[]{:S(2)}, u32[]{:S(2)}) collective-permute-start(bf16[1,10,2048]{2,1,0:T(8,128)(2,1)S(1)} %get-tuple-element.36), channel_id=1, source_target_pairs={{0,7},{1,0},{2,1},{3,2},{4,3},{5,4},{6,5},{7,6},{8,15},{9,8},{10,9... | collective-permute-start | bytes 122888 | tf_op jit(solution)/shard_map/ppermute | solution.py:36
  199.2 2.9 %collective-permute-start.20 = (bf16[1,10,2048]{2,1,0:T(8,128)(2,1)S(1)}, bf16[1,10,2048]{2,1,0:T(8,128)(2,1)S(1)}, u32[]{:S(2)}, u32[]{:S(2)}) collective-permute-start(bf16[1,10,2048]{2,1,0:T(8,128)(2,1)S(1)} %get-tuple-element.39), channel_id=1, source_target_pairs={{0,4},{1,5},{2,6},{3,7},{4,0},{5,1},{6,2},{7,3},{8,12},{9,13},{10,... | collective-permute-start | bytes 122888 | tf_op jit(solution)/shard_map/ppermute | solution.py:36
  202.3 5.9 %collective-permute-done.18 = bf16[1,10,2048]{2,1,0:T(8,128)(2,1)S(1)} collective-permute-done((bf16[1,10,2048]{2,1,0:T(8,128)(2,1)S(1)}, bf16[1,10,2048]{2,1,0:T(8,128)(2,1)S(1)}, u32[]{:S(2)}, u32[]{:S(2)}) %collective-permute-start.18) | collective-permute-done | bytes 40992 | tf_op jit(solution)/shard_map/ppermute | solution.py:36
  208.5 6.5 %collective-permute-done.19 = bf16[1,10,2048]{2,1,0:T(8,128)(2,1)S(1)} collective-permute-done((bf16[1,10,2048]{2,1,0:T(8,128)(2,1)S(1)}, bf16[1,10,2048]{2,1,0:T(8,128)(2,1)S(1)}, u32[]{:S(2)}, u32[]{:S(2)}) %collective-permute-start.19) | collective-permute-done | bytes 40992 | tf_op jit(solution)/shard_map/ppermute | solution.py:36
  215.1 0.6 gather_fusion.1
  216.1 8.4 %all_to_all.34 = bf16[8,8,2048]{2,1,0:T(8,128)(2,1)S(1)} all-to-all(bf16[8,8,2048]{2,1,0:T(8,128)(2,1)S(1)} %fusion.17), channel_id=1, replica_groups=mesh['roll'=4,'tp'=8] {'roll'}, dimensions={0} | all-to-all | bytes 524288 | tf_op jit(solution)/shard_map/all_to_all | solution.py:158
  225.0 0.7 copy.33
  (156 shorter events, 12.2 us)
Async XLA Ops:
  3.2 14.7 %all-to-all-start = ((s32[4,1,12]{2,1,0:T(1,128)}), s32[4,1,12]{2,1,0:T(1,128)S(1)}, u32[]{:S(2)}, u32[]{:S(2)}) async-start(s32[4,1,12]{2,1,0:T(1,128)} %broadcast_in_dim.29), calls=%async_computation | async-start | bytes 4096 | tf_op jit(solution)/shard_map/all_to_all | solution.py:119
  7.5 4.6 %copy-start.1 = (f32[1,1,2048,768]{3,2,1,0:T(8,128)S(1)}, f32[1,1,2048,768]{3,2,1,0:T(8,128)}, u32[]{:S(2)}) copy-start(f32[1,1,2048,768]{3,2,1,0:T(8,128)} %param.13) | copy-start | bytes 18874372
  9.7 1.4 copy-start
  11.2 12.1 %collective-permute-start.1 = (bf16[192,2048]{1,0:T(8,128)(2,1)}, bf16[192,2048]{1,0:T(8,128)(2,1)}, u32[]{:S(2)}, u32[]{:S(2)}) collective-permute-start(bf16[192,2048]{1,0:T(8,128)(2,1)} %select_bitcast_fusion.1), channel_id=1, source_target_pairs={{0,8},{8,0},{16,24},{24,16},{1,9},{9,1},{17,25},{25,17},{2,10},{10... | collective-permute-start | bytes 2359304 | tf_op jit(solution)/shard_map/ppermute | solution.py:73
  12.3 1.9 copy-start.17
  12.4 1.9 copy-start.20
  12.4 2.1 copy-start.23
  12.4 5.4 %copy-start.12 = (bf16[4,8,2048]{2,1,0:T(8,128)(2,1)S(1)}, bf16[4,8,2048]{2,1,0:T(8,128)(2,1)}, u32[]{:S(2)}) copy-start(bf16[4,8,2048]{2,1,0:T(8,128)(2,1)} %param.9) | copy-start | bytes 393220
  13.7 12.5 %collective-permute-start = (bf16[1024,768]{1,0:T(8,128)(2,1)}, bf16[1024,768]{1,0:T(8,128)(2,1)}, u32[]{:S(2)}, u32[]{:S(2)}) collective-permute-start(bf16[1024,768]{1,0:T(8,128)(2,1)} %select_bitcast_fusion), channel_id=1, source_target_pairs={{0,8},{8,0},{16,24},{24,16},{1,9},{9,1},{17,25},{25,17},{2,10},{10... | collective-permute-start | bytes 4718600 | tf_op jit(solution)/shard_map/ppermute | solution.py:73
  14.5 17.6 %copy-start.18 = (s32[64]{0:T(128)}, s32[64]{0:T(128)S(1)}, u32[]{:S(2)}) copy-start(s32[64]{0:T(128)S(1)} %get-tuple-element.65) | copy-start | bytes 772
  19.9 9.8 %all-to-all-start.1 = ((bf16[8,8,2048]{2,1,0:T(8,128)(2,1)}), bf16[8,8,2048]{2,1,0:T(8,128)(2,1)S(1)}, u32[]{:S(2)}, u32[]{:S(2)}) async-start(bf16[8,8,2048]{2,1,0:T(8,128)(2,1)} %copy.15), calls=%async_computation.1 | async-start | bytes 524288 | tf_op jit(solution)/shard_map/all_to_all | solution.py:206
  26.3 5.4 %copy-start.16 = (f32[2,2048]{1,0:T(2,128)S(1)}, f32[2,2048]{1,0:T(2,128)}, u32[]{:S(2)}) copy-start(f32[2,2048]{1,0:T(2,128)} %param.15) | copy-start | bytes 49156
  29.6 54.7 %copy-start.3 = (bf16[1024,768]{1,0:T(8,128)(2,1)S(1)}, bf16[1024,768]{1,0:T(8,128)(2,1)}, u32[]{:S(2)}) copy-start(bf16[1024,768]{1,0:T(8,128)(2,1)} %get-tuple-element.12) | copy-start | bytes 4718596
  29.6 54.7 %collective-permute-start.2 = (bf16[1024,768]{1,0:T(8,128)(2,1)}, bf16[1024,768]{1,0:T(8,128)(2,1)}, u32[]{:S(2)}, u32[]{:S(2)}) collective-permute-start(bf16[1024,768]{1,0:T(8,128)(2,1)} %get-tuple-element.12), channel_id=1, source_target_pairs={{0,16},{8,24},{16,0},{24,8},{1,17},{9,25},{17,1},{25,9},{2,18},{10... | collective-permute-start | bytes 4718600 | tf_op jit(solution)/shard_map/ppermute | solution.py:73
  32.0 51.5 %collective-permute-start.3 = (bf16[192,2048]{1,0:T(8,128)(2,1)}, bf16[192,2048]{1,0:T(8,128)(2,1)S(1)}, u32[]{:S(2)}, u32[]{:S(2)}) collective-permute-start(bf16[192,2048]{1,0:T(8,128)(2,1)} %get-tuple-element.13), channel_id=1, source_target_pairs={{0,16},{8,24},{16,0},{24,8},{1,17},{9,25},{17,1},{25,9},{2,18},{10... | collective-permute-start | bytes 2359304 | tf_op jit(solution)/shard_map/ppermute | solution.py:73
  33.3 20.9 %all-to-all-start.2 = ((bf16[8,10,2048]{2,1,0:T(8,128)(2,1)}), bf16[8,10,2048]{2,1,0:T(8,128)(2,1)}, u32[]{:S(2)}, u32[]{:S(2)}) async-start(bf16[8,10,2048]{2,1,0:T(8,128)(2,1)} %reshape.275), calls=%async_computation.2 | async-start | bytes 1048576 | tf_op jit(solution)/shard_map/all_to_all | solution.py:178
  54.2 32.4 %copy-start.4 = (bf16[192,2048]{1,0:T(8,128)(2,1)S(1)}, bf16[192,2048]{1,0:T(8,128)(2,1)}, u32[]{:S(2)}) copy-start(bf16[192,2048]{1,0:T(8,128)(2,1)} %get-tuple-element.13) | copy-start | bytes 2359300
  83.5 0.9 copy-start.5
  84.3 2.3 %copy-start.6 = (bf16[192,2048]{1,0:T(8,128)(2,1)S(1)}, bf16[192,2048]{1,0:T(8,128)(2,1)}, u32[]{:S(2)}) copy-start(bf16[192,2048]{1,0:T(8,128)(2,1)} %copy-done.5) | copy-start | bytes 2359300
  86.2 3.6 %copy-start.27 = (f32[2,64]{1,0:T(2,128)S(1)}, f32[2,64]{1,0:T(2,128)}, u32[]{:S(2)}) copy-start(f32[2,64]{1,0:T(2,128)} %param.17) | copy-start | bytes 1540
  86.2 9.2 %collective-permute-start.4 = (bf16[1024,768]{1,0:T(8,128)(2,1)S(1)}, bf16[1024,768]{1,0:T(8,128)(2,1)}, u32[]{:S(2)}, u32[]{:S(2)}) collective-permute-start(bf16[1024,768]{1,0:T(8,128)(2,1)S(1)} %add.223), channel_id=1, source_target_pairs={{0,8},{8,0},{16,24},{24,16},{1,9},{9,1},{17,25},{25,17},{2,10},{10... | collective-permute-start | bytes 4718600 | tf_op jit(solution)/shard_map/ppermute | solution.py:73
  86.6 5.6 %copy-start.24 = (s32[4]{0:T(128)}, s32[4]{0:T(128)S(1)}, u32[]{:S(2)}) copy-start(s32[4]{0:T(128)S(1)} %get-tuple-element.21) | copy-start | bytes 52
  86.7 5.6 %copy-start.2 = (bf16[1024,768]{1,0:T(8,128)(2,1)S(1)}, bf16[1024,768]{1,0:T(8,128)(2,1)}, u32[]{:S(2)}) copy-start(bf16[1024,768]{1,0:T(8,128)(2,1)} %get-tuple-element.17) | copy-start | bytes 4718596
  87.8 6.1 %collective-permute-start.5 = (bf16[192,2048]{1,0:T(8,128)(2,1)}, bf16[192,2048]{1,0:T(8,128)(2,1)}, u32[]{:S(2)}, u32[]{:S(2)}) collective-permute-start(bf16[192,2048]{1,0:T(8,128)(2,1)} %add.225), channel_id=1, source_target_pairs={{0,8},{8,0},{16,24},{24,16},{1,9},{9,1},{17,25},{25,17},{2,10},{10... | collective-permute-start | bytes 2359304 | tf_op jit(solution)/shard_map/ppermute | solution.py:73
  92.2 37.4 %collective-permute-start.13 = (bf16[1024,768]{1,0:T(8,128)(2,1)S(1)}, bf16[1024,768]{1,0:T(8,128)(2,1)}, u32[]{:S(2)}, u32[]{:S(2)}) collective-permute-start(bf16[1024,768]{1,0:T(8,128)(2,1)S(1)} %copy-done.2), channel_id=1, source_target_pairs={{0,16},{8,24},{16,0},{24,8},{1,17},{9,25},{17,1},{25,9},{2,18},{10... | collective-permute-start | bytes 4718600 | tf_op jit(solution)/shard_map/ppermute | solution.py:73
  95.4 1.7 copy-start.11
  99.0 36.4 %collective-permute-start.6 = (bf16[1,10,2048]{2,1,0:T(8,128)(2,1)}, bf16[1,10,2048]{2,1,0:T(8,128)(2,1)}, u32[]{:S(2)}, u32[]{:S(2)}) collective-permute-start(bf16[1,10,2048]{2,1,0:T(8,128)(2,1)} %get-tuple-element.50), channel_id=1, source_target_pairs={{0,1},{1,2},{2,3},{3,4},{4,5},{5,6},{6,7},{7,0},{8,9},{9,10},{10,1... | collective-permute-start | bytes 122888 | tf_op jit(solution)/shard_map/ppermute | solution.py:36
  102.7 58.1 %collective-permute-start.15 = (bf16[192,2048]{1,0:T(8,128)(2,1)}, bf16[192,2048]{1,0:T(8,128)(2,1)}, u32[]{:S(2)}, u32[]{:S(2)}) collective-permute-start(bf16[192,2048]{1,0:T(8,128)(2,1)} %get-tuple-element.18), channel_id=1, source_target_pairs={{0,16},{8,24},{16,0},{24,8},{1,17},{9,25},{17,1},{25,9},{2,18},{10... | collective-permute-start | bytes 2359304 | tf_op jit(solution)/shard_map/ppermute | solution.py:73
  103.1 49.9 %collective-permute-start.12 = (bf16[1,10,2048]{2,1,0:T(8,128)(2,1)S(1)}, bf16[1,10,2048]{2,1,0:T(8,128)(2,1)S(1)}, u32[]{:S(2)}, u32[]{:S(2)}) collective-permute-start(bf16[1,10,2048]{2,1,0:T(8,128)(2,1)S(1)} %get-tuple-element.44), channel_id=1, source_target_pairs={{0,7},{1,0},{2,1},{3,2},{4,3},{5,4},{6,5},{7,6},{8,15},{9,8},{10,9... | collective-permute-start | bytes 122888 | tf_op jit(solution)/shard_map/ppermute | solution.py:36
  106.2 46.9 %collective-permute-start.11 = (bf16[1,10,2048]{2,1,0:T(8,128)(2,1)S(1)}, bf16[1,10,2048]{2,1,0:T(8,128)(2,1)S(1)}, u32[]{:S(2)}, u32[]{:S(2)}) collective-permute-start(bf16[1,10,2048]{2,1,0:T(8,128)(2,1)S(1)} %get-tuple-element.45), channel_id=1, source_target_pairs={{0,6},{1,7},{2,0},{3,1},{4,2},{5,3},{6,4},{7,5},{8,14},{9,15},{10,... | collective-permute-start | bytes 122888 | tf_op jit(solution)/shard_map/ppermute | solution.py:36
  129.6 5.9 %copy-start.15 = (bf16[1,10,2048]{2,1,0:T(8,128)(2,1)S(1)}, bf16[1,10,2048]{2,1,0:T(8,128)(2,1)}, u32[]{:S(2)}) copy-start(bf16[1,10,2048]{2,1,0:T(8,128)(2,1)} %get-tuple-element.49) | copy-start | bytes 122884
  129.6 7.5 %copy-start.9 = (bf16[8,1,10,2048]{3,2,0,1:T(8,128)(2,1)S(1)}, bf16[8,1,10,2048]{3,2,0,1:T(8,128)(2,1)}, u32[]{:S(2)}) copy-start(bf16[8,1,10,2048]{3,2,0,1:T(8,128)(2,1)} %get-tuple-element.51) | copy-start | bytes 983044
  129.6 12.0 %copy-start.14 = (bf16[1,10,2048]{2,1,0:T(8,128)(2,1)S(1)}, bf16[1,10,2048]{2,1,0:T(8,128)(2,1)}, u32[]{:S(2)}) copy-start(bf16[1,10,2048]{2,1,0:T(8,128)(2,1)} %get-tuple-element.48) | copy-start | bytes 122884
  129.6 18.2 %copy-start.13 = (bf16[1,10,2048]{2,1,0:T(8,128)(2,1)S(1)}, bf16[1,10,2048]{2,1,0:T(8,128)(2,1)}, u32[]{:S(2)}) copy-start(bf16[1,10,2048]{2,1,0:T(8,128)(2,1)} %get-tuple-element.47) | copy-start | bytes 122884
  129.6 23.4 %collective-permute-start.10 = (bf16[1,10,2048]{2,1,0:T(8,128)(2,1)}, bf16[1,10,2048]{2,1,0:T(8,128)(2,1)S(1)}, u32[]{:S(2)}, u32[]{:S(2)}) collective-permute-start(bf16[1,10,2048]{2,1,0:T(8,128)(2,1)} %get-tuple-element.46), channel_id=1, source_target_pairs={{0,5},{1,6},{2,7},{3,0},{4,1},{5,2},{6,3},{7,4},{8,13},{9,14},{10,... | collective-permute-start | bytes 122888 | tf_op jit(solution)/shard_map/ppermute | solution.py:36
  135.4 20.2 %copy-start.19 = (s32[64]{0:T(128)S(1)}, s32[64]{0:T(128)}, u32[]{:S(2)}) copy-start(s32[64]{0:T(128)} %copy-done.18) | copy-start | bytes 772
  135.4 20.2 %copy-start.26 = (f32[64]{0:T(128)S(1)}, f32[64]{0:T(128)}, u32[]{:S(2)}) copy-start(f32[64]{0:T(128)} %get-tuple-element.63) | copy-start | bytes 772
  135.5 6.1 %collective-permute-start.7 = (bf16[1,10,2048]{2,1,0:T(8,128)(2,1)S(1)}, bf16[1,10,2048]{2,1,0:T(8,128)(2,1)S(1)}, u32[]{:S(2)}, u32[]{:S(2)}) collective-permute-start(bf16[1,10,2048]{2,1,0:T(8,128)(2,1)S(1)} %copy-done.15), channel_id=1, source_target_pairs={{0,2},{1,3},{2,4},{3,5},{4,6},{5,7},{6,0},{7,1},{8,10},{9,11},{10,... | collective-permute-start | bytes 122888 | tf_op jit(solution)/shard_map/ppermute | solution.py:36
  141.6 6.2 %collective-permute-start.8 = (bf16[1,10,2048]{2,1,0:T(8,128)(2,1)S(1)}, bf16[1,10,2048]{2,1,0:T(8,128)(2,1)S(1)}, u32[]{:S(2)}, u32[]{:S(2)}) collective-permute-start(bf16[1,10,2048]{2,1,0:T(8,128)(2,1)S(1)} %copy-done.14), channel_id=1, source_target_pairs={{0,3},{1,4},{2,5},{3,6},{4,7},{5,0},{6,1},{7,2},{8,11},{9,12},{10,... | collective-permute-start | bytes 122888 | tf_op jit(solution)/shard_map/ppermute | solution.py:36
  147.8 5.2 %collective-permute-start.9 = (bf16[1,10,2048]{2,1,0:T(8,128)(2,1)S(1)}, bf16[1,10,2048]{2,1,0:T(8,128)(2,1)S(1)}, u32[]{:S(2)}, u32[]{:S(2)}) collective-permute-start(bf16[1,10,2048]{2,1,0:T(8,128)(2,1)S(1)} %copy-done.13), channel_id=1, source_target_pairs={{0,4},{1,5},{2,6},{3,7},{4,0},{5,1},{6,2},{7,3},{8,12},{9,13},{10,... | collective-permute-start | bytes 122888 | tf_op jit(solution)/shard_map/ppermute | solution.py:36
  153.0 37.7 %collective-permute-start.14 = (bf16[1024,768]{1,0:T(8,128)(2,1)S(1)}, bf16[1024,768]{1,0:T(8,128)(2,1)}, u32[]{:S(2)}, u32[]{:S(2)}) collective-permute-start(bf16[1024,768]{1,0:T(8,128)(2,1)S(1)} %add.253), channel_id=1, source_target_pairs={{0,8},{8,0},{16,24},{24,16},{1,9},{9,1},{17,25},{25,17},{2,10},{10... | collective-permute-start | bytes 4718600 | tf_op jit(solution)/shard_map/ppermute | solution.py:73
  153.1 0.8 copy-start.10
  153.9 2.3 %copy-start.28 = (s32[4]{0:T(128)S(1)}, s32[4]{0:T(128)}, u32[]{:S(2)}) copy-start(s32[4]{0:T(128)} %compare_select_fusion.3) | copy-start | bytes 52
  155.7 5.1 %copy-start.25 = (s32[4]{0:T(128)S(1)}, s32[4]{0:T(128)}, u32[]{:S(2)}) copy-start(s32[4]{0:T(128)} %copy-done.24) | copy-start | bytes 52
  157.3 9.4 %all-to-all-start.3 = ((bf16[4,2,8,2048]{3,2,1,0:T(8,128)(2,1)}), bf16[4,2,8,2048]{3,2,1,0:T(8,128)(2,1)S(1)}, u32[]{:S(2)}, u32[]{:S(2)}) async-start(bf16[4,2,8,2048]{3,2,1,0:T(8,128)(2,1)} %bitcast.138), calls=%async_computation.3 | async-start | bytes 524288 | tf_op jit(solution)/shard_map/all_to_all | solution.py:153
  162.4 12.6 %collective-permute-start.16 = (bf16[192,2048]{1,0:T(8,128)(2,1)S(1)}, bf16[192,2048]{1,0:T(8,128)(2,1)}, u32[]{:S(2)}, u32[]{:S(2)}) collective-permute-start(bf16[192,2048]{1,0:T(8,128)(2,1)S(1)} %add.255), channel_id=1, source_target_pairs={{0,8},{8,0},{16,24},{24,16},{1,9},{9,1},{17,25},{25,17},{2,10},{10... | collective-permute-start | bytes 2359304 | tf_op jit(solution)/shard_map/ppermute | solution.py:73
  170.9 18.7 %all-to-all-start.4 = ((bf16[8,10,2048]{2,1,0:T(8,128)(2,1)}), bf16[8,10,2048]{2,1,0:T(8,128)(2,1)}, u32[]{:S(2)}, u32[]{:S(2)}) async-start(bf16[8,10,2048]{2,1,0:T(8,128)(2,1)} %reshape.279), calls=%async_computation.4 | async-start | bytes 1048576 | tf_op jit(solution)/shard_map/all_to_all | solution.py:178
  192.4 1.1 copy-start.7
  192.4 1.4 copy-start.8
  194.4 21.5 %copy-start.21 = (f32[64]{0:T(128)S(1)}, f32[64]{0:T(128)}, u32[]{:S(2)}) copy-start(f32[64]{0:T(128)} %get-tuple-element.62) | copy-start | bytes 772
  194.4 7.7 %collective-permute-start.17 = (bf16[1,10,2048]{2,1,0:T(8,128)(2,1)S(1)}, bf16[1,10,2048]{2,1,0:T(8,128)(2,1)S(1)}, u32[]{:S(2)}, u32[]{:S(2)}) collective-permute-start(bf16[1,10,2048]{2,1,0:T(8,128)(2,1)S(1)} %get-tuple-element.42), channel_id=1, source_target_pairs={{0,1},{1,2},{2,3},{3,4},{4,5},{5,6},{6,7},{7,0},{8,9},{9,10},{10,1... | collective-permute-start | bytes 122888 | tf_op jit(solution)/shard_map/ppermute | solution.py:36
  195.9 19.2 %collective-permute-start.23 = (bf16[1,10,2048]{2,1,0:T(8,128)(2,1)S(1)}, bf16[1,10,2048]{2,1,0:T(8,128)(2,1)S(1)}, u32[]{:S(2)}, u32[]{:S(2)}) collective-permute-start(bf16[1,10,2048]{2,1,0:T(8,128)(2,1)S(1)} %get-tuple-element.36), channel_id=1, source_target_pairs={{0,7},{1,0},{2,1},{3,2},{4,3},{5,4},{6,5},{7,6},{8,15},{9,8},{10,9... | collective-permute-start | bytes 122888 | tf_op jit(solution)/shard_map/ppermute | solution.py:36
  199.2 15.9 %collective-permute-start.22 = (bf16[1,10,2048]{2,1,0:T(8,128)(2,1)S(1)}, bf16[1,10,2048]{2,1,0:T(8,128)(2,1)S(1)}, u32[]{:S(2)}, u32[]{:S(2)}) collective-permute-start(bf16[1,10,2048]{2,1,0:T(8,128)(2,1)S(1)} %get-tuple-element.37), channel_id=1, source_target_pairs={{0,6},{1,7},{2,0},{3,1},{4,2},{5,3},{6,4},{7,5},{8,14},{9,15},{10,... | collective-permute-start | bytes 122888 | tf_op jit(solution)/shard_map/ppermute | solution.py:36
  199.2 15.9 %collective-permute-start.21 = (bf16[1,10,2048]{2,1,0:T(8,128)(2,1)S(1)}, bf16[1,10,2048]{2,1,0:T(8,128)(2,1)S(1)}, u32[]{:S(2)}, u32[]{:S(2)}) collective-permute-start(bf16[1,10,2048]{2,1,0:T(8,128)(2,1)S(1)} %get-tuple-element.38), channel_id=1, source_target_pairs={{0,5},{1,6},{2,7},{3,0},{4,1},{5,2},{6,3},{7,4},{8,13},{9,14},{10,... | collective-permute-start | bytes 122888 | tf_op jit(solution)/shard_map/ppermute | solution.py:36
  199.2 15.9 %collective-permute-start.20 = (bf16[1,10,2048]{2,1,0:T(8,128)(2,1)S(1)}, bf16[1,10,2048]{2,1,0:T(8,128)(2,1)S(1)}, u32[]{:S(2)}, u32[]{:S(2)}) collective-permute-start(bf16[1,10,2048]{2,1,0:T(8,128)(2,1)S(1)} %get-tuple-element.39), channel_id=1, source_target_pairs={{0,4},{1,5},{2,6},{3,7},{4,0},{5,1},{6,2},{7,3},{8,12},{9,13},{10,... | collective-permute-start | bytes 122888 | tf_op jit(solution)/shard_map/ppermute | solution.py:36
  202.1 6.2 %collective-permute-start.18 = (bf16[1,10,2048]{2,1,0:T(8,128)(2,1)S(1)}, bf16[1,10,2048]{2,1,0:T(8,128)(2,1)S(1)}, u32[]{:S(2)}, u32[]{:S(2)}) collective-permute-start(bf16[1,10,2048]{2,1,0:T(8,128)(2,1)S(1)} %get-tuple-element.41), channel_id=1, source_target_pairs={{0,2},{1,3},{2,4},{3,5},{4,6},{5,7},{6,0},{7,1},{8,10},{9,11},{10,... | collective-permute-start | bytes 122888 | tf_op jit(solution)/shard_map/ppermute | solution.py:36
  208.3 6.8 %collective-permute-start.19 = (bf16[1,10,2048]{2,1,0:T(8,128)(2,1)S(1)}, bf16[1,10,2048]{2,1,0:T(8,128)(2,1)S(1)}, u32[]{:S(2)}, u32[]{:S(2)}) collective-permute-start(bf16[1,10,2048]{2,1,0:T(8,128)(2,1)S(1)} %get-tuple-element.40), channel_id=1, source_target_pairs={{0,3},{1,4},{2,5},{3,6},{4,7},{5,0},{6,1},{7,2},{8,11},{9,12},{10,... | collective-permute-start | bytes 122888 | tf_op jit(solution)/shard_map/ppermute | solution.py:36
  215.7 9.0 %copy-start.22 = (s32[4]{0:T(128)S(1)}, s32[4]{0:T(128)}, u32[]{:S(2)}) copy-start(s32[4]{0:T(128)} %get-tuple-element.58) | copy-start | bytes 52
